TPU v7x, 512 devices: a whole 4x4x16 slice. The times are simulated.
512 devices in a mesh: dp: 2 (over core), expert: 16 (over z_hi, x), seg: 16 (over z_lo, y).
Axes of the slice: x: 4, y: 4, z: 16 (z_hi: 4, z_lo: 4; z = z_hi * 4 + z_lo), core: 2. Of those that a mesh axis runs over, the one named last changes fastest.
Arguments:
- tokens: bfloat16 [2048, 3072], P(('dp', 'expert'), 'seg'), parts along dimension 0, may hold values from -6 to 6
- expert_ids: int32 [2048, 4], P(('dp', 'expert')), parts along dimension 0, may hold values from 0 to 15, as said below
- route_weight: float32 [2048, 4], P(('dp', 'expert')), parts along dimension 0, may hold values from 0.1 to 1
- w_up: bfloat16 [16, 3072, 6144], P('expert', None, 'seg'), may hold values from -0.109375 to 0.109375
- w_down: bfloat16 [16, 6144, 3072], P('expert', 'seg'), may hold values from -0.078125 to 0.078125
Outputs:
- mixed: bfloat16 [2048, 3072], P(('dp', 'expert'), 'seg'), parts along dimension 0
There are 2 independent parts, one for each index of `dp`. A program takes and returns all parts, laid end to end along the dimension named above; an argument that names none is the same for every part. Nothing has to cross between parts.
Inputs may be any that keep to these rules, and one draw needn't show every extreme that they name: `expert_ids`: each row names 4 different experts. Within each aligned block of 64 rows (the rows of one device), no expert is named by more than 21 rows, and one expert is named by exactly 21 rows in every block.
All inputs are finite; a program needn't handle non-finite values.
Results may differ from a plain program's by a relative error of at most 0.0049.
Values may be sent and summed in bfloat16 or wider, within the bound.
A program may use at most 64 MiB of HBM per device.

v0:
```python
import jax
import jax.numpy as jnp
from jax import lax
from jax.sharding import PartitionSpec as P

EXPERTS = 16
SEND_CAP = 21


def route_slots(expert_ids):
    flat_route = expert_ids.reshape(-1)
    onehot = (flat_route[:, None] == jnp.arange(EXPERTS, dtype=jnp.int32)[None, :]).astype(
        jnp.int32
    )
    before = jnp.cumsum(onehot, axis=0) - onehot
    return flat_route * SEND_CAP + jnp.sum(before * onehot, axis=1)


def pack_rows(rows, target, topk):
    repeated = jnp.repeat(rows, topk, axis=0)
    buffer = jnp.zeros((EXPERTS * SEND_CAP, rows.shape[1]), rows.dtype)
    return buffer.at[target].set(repeated)


def shards(tokens, expert_ids, route_weight, w_up, w_down):
    expert_count = lax.axis_size("expert")
    exp_local = w_up.shape[0]
    topk = expert_ids.shape[1]
    tok_rows = tokens.shape[0]
    width_seg = tokens.shape[1]
    target = route_slots(expert_ids)
    norm_weight = route_weight / jnp.sum(route_weight, axis=1, keepdims=True)
    flat_weight = norm_weight.reshape(-1)
    packed = pack_rows(tokens, target, topk).reshape(expert_count, exp_local * SEND_CAP, width_seg)
    arrived = lax.all_to_all(packed, "expert", split_axis=0, concat_axis=0, tiled=True)
    piece = lax.all_gather(arrived, "seg", axis=2, tiled=True)
    block = piece.reshape(piece.shape[0], exp_local, SEND_CAP, piece.shape[2])
    up_sum = jnp.einsum("sekd,edf->eskf", block, w_up, preferred_element_type=jnp.float32)
    hidden = jax.nn.silu(up_sum).astype(jnp.bfloat16)
    source_count = hidden.shape[1]
    term = jnp.einsum("efc,eskf->csek", w_down, hidden, preferred_element_type=jnp.float32)
    summed = lax.psum_scatter(
        term.reshape(width_seg * lax.axis_size("seg"), source_count, exp_local * SEND_CAP),
        "seg",
        scatter_dimension=0,
        tiled=True,
    )
    returned = lax.all_to_all(summed, "expert", split_axis=1, concat_axis=1, tiled=True)
    picked = returned.reshape(width_seg, EXPERTS * SEND_CAP)[:, target]
    weighted = (picked * flat_weight[None, :]).reshape(width_seg, tok_rows, topk).sum(axis=2)
    return weighted.T.astype(jnp.bfloat16)


def solution(mesh):
    placed = (
        P(("dp", "expert"), "seg"),
        P(("dp", "expert"), None),
        P(("dp", "expert"), None),
        P("expert", None, "seg"),
        P("expert", "seg", None),
    )
    return jax.shard_map(
        shards, mesh=mesh, in_specs=placed, out_specs=P(("dp", "expert"), "seg"), check_vma=False
    )
```

profile of v0, /device:TPU:2, one launch (start us, length us, event | category | flops | bytes accessed | tf_op | source)
XLA Modules:
  0.0 354.8 jit_solution(8513989447050514954)
XLA Ops:
  6.5 0.0 copy-start
  6.5 0.0 all-gather.2.cloned.1.call-start
  6.5 0.9 copy.13
  7.5 0.1 eq.29
  7.6 0.1 eq.25
  7.7 0.7 broadcast_multiply_fusion
  8.4 0.6 reduce-window.6
  8.9 0.2 slice_reduce_fusion
  9.2 0.1 copy.12
  9.3 0.1 mul.35
  9.4 0.8 broadcast_in_dim.5
  10.2 0.1 reshape.105
  10.3 0.1 fusion.17
  10.4 1.5 scatter_custom_fusion
  11.9 0.1 reshape.88
  11.9 35.1 %all_to_all.10 = bf16[16,21,192]{2,1,0:T(8,128)(2,1)S(1)} all-to-all(bf16[16,21,192]{2,1,0:T(8,128)(2,1)S(1)} %reshape.88), channel_id=1, replica_groups=mesh['dp'=2,'expert'=16,'seg'=16] {'expert'}, dimensions={0} | all-to-all | bytes 258048 | tf_op jit(solution)/shard_map/all_to_all | solution.py:35
  47.0 1.6 copy.16
  48.6 0.0 all-gather.2.cloned.1.call-update
  48.6 0.0 reduce-scatter.4.cloned.1.call-start
  48.7 143.6 %all-gather.2.cloned.1.call-done = bf16[16,21,3072]{1,0,2:T(8,128)(2,1)} async-done(((bf16[16,21,192]{1,0,2:T(8,128)(2,1)}), bf16[16,21,3072]{1,0,2:T(8,128)(2,1)}) %all-gather.2.cloned.1.call-update) | async-done | bytes 2064400 | tf_op jit(solution)/shard_map/all_gather | solution.py:36
  192.2 0.0 copy-done
  192.2 12.3 %convolution_bitcast_fusion = f32[3072,16,21]{0,2,1:T(8,128)} fusion(bf16[1,384,3072]{2,1,0:T(8,128)(2,1)S(1)} %copy-done, bf16[1,3072,384]{2,1,0:T(8,128)(2,1)} %param.8, bf16[16,21,3072]{1,0,2:T(8,128)(2,1)} %all-gather.2.cloned.1.call-done), kind=kOutput, calls=%fused_computation.4 | convolution fusion | flops 1586092032 | bytes 10911744 | tf_op jit(solution)/shard_map/efc,eskf->csek/dot_general | solution.py:41
  204.5 4.0 %reshape.113 = f32[3072,336]{0,1:T(8,128)} reshape(f32[3072,16,21]{0,2,1:T(8,128)} %convolution_bitcast_fusion) | data formatting | bytes 8257536
  208.5 5.8 %copy.21 = f32[3072,336]{1,0:T(8,128)} copy(f32[3072,336]{0,1:T(8,128)} %reshape.113) | data formatting | bytes 8257536
  214.3 0.0 copy-start.1
  214.3 0.0 reduce-scatter.4.cloned.1.call-update
  214.3 97.9 %reduce-scatter.4.cloned.1.call-done = f32[192,336]{1,0:T(8,128)} async-done(((f32[3072,336]{1,0:T(8,128)}), f32[192,336]{1,0:T(8,128)}) %reduce-scatter.4.cloned.1.call-update) | async-done | bytes 258064
  312.3 3.1 reshape.112
  315.4 2.9 copy.20
  318.2 12.4 %all-to-all-start.1 = ((f32[192,16,21]{0,2,1:T(8,128)}), f32[192,16,21]{0,2,1:T(8,128)S(1)}, u32[]{:S(2)}, u32[]{:S(2)}) async-start(f32[192,16,21]{0,2,1:T(8,128)} %copy.20), calls=%async_computation.1 | async-start | bytes 786432 | tf_op jit(solution)/shard_map/all_to_all | solution.py:48
  330.7 0.0 copy-done.1
  330.7 0.1 copy.18
  330.8 15.1 %all-to-all-done.1 = f32[192,16,21]{0,2,1:T(8,128)S(1)} async-done(((f32[192,16,21]{0,2,1:T(8,128)}), f32[192,16,21]{0,2,1:T(8,128)S(1)}, u32[]{:S(2)}, u32[]{:S(2)}) %all-to-all-start.1) | async-done | bytes 258080 | tf_op jit(solution)/shard_map/all_to_all | solution.py:48
  346.0 1.0 gather_fusion
  347.0 0.1 gather.6
  347.1 0.9 multiply_reduce_fusion
  (8 shorter events, 0.1 us)
Async XLA Ops:
  6.5 185.7 %copy-start = (bf16[1,384,3072]{2,1,0:T(8,128)(2,1)S(1)}, bf16[1,384,3072]{2,1,0:T(8,128)(2,1)}, u32[]{:S(2)}) copy-start(bf16[1,384,3072]{2,1,0:T(8,128)(2,1)} %param.9) | copy-start | bytes 7077892
  6.5 185.7 %all-gather.2.cloned.1.call-start = ((), (), s32[]{:S(2)}) async-start(), calls=%async_computation.3 | async-start | bytes 13369344 | tf_op jit(solution)/shard_map/all_gather | solution.py:36
  48.6 263.7 %reduce-scatter.4.cloned.1.call-start = ((), (), s32[]{:S(2)}) async-start(), calls=%async_computation.4 | async-start | bytes 5013504
  214.3 116.4 %copy-start.1 = (f32[64,4]{0,1:T(4,128)S(1)}, f32[64,4]{0,1:T(4,128)}, u32[]{:S(2)}) copy-start(f32[64,4]{0,1:T(4,128)} %param.7) | copy-start | bytes 3076
  318.2 27.7 %all-to-all-start.1 = ((f32[192,16,21]{0,2,1:T(8,128)}), f32[192,16,21]{0,2,1:T(8,128)S(1)}, u32[]{:S(2)}, u32[]{:S(2)}) async-start(f32[192,16,21]{0,2,1:T(8,128)} %copy.20), calls=%async_computation.1 | async-start | bytes 786432 | tf_op jit(solution)/shard_map/all_to_all | solution.py:48
Sparse Core Ops, SparseCore 0:
  48.7 143.4 all-gather.1
  214.5 97.7 reduce-scatter.3
where the time goes:
time: 355 us
  waiting for transfers between devices  257 us (72%)
  blocking collectives  35.1 us (10%)
  local copies, waits for them, and re-layouts  22.5 us (6%)
  between operations  13.5 us (4%)
  starting transfers between devices  12.5 us (4%)
  matrix products  12.3 us (3%)
    all_gather x1, waiting for transfers between devices, shards(): piece = lax.all_gather(arrived, 'seg', axis=2, tiled=True)  144 us
    unnamed x3, waiting for transfers between devices  98 us
    all_to_all x1, blocking collectives, shards(): lax.all_to_all(packed, 'expert', split_axis=0, concat_axis=0, tiled=True)  35.1 us
    unnamed x9, local copies, waits for them, and re-layouts  16.7 us
    all_to_all x1, waiting for transfers between devices, shards(): lax.all_to_all(summed, 'expert', split_axis=1, concat_axis=1, tiled=True)  15.1 us
    all_to_all x1, starting transfers between devices, shards(): lax.all_to_all(summed, 'expert', split_axis=1, concat_axis=1, tiled=True)  12.4 us
    dot_general x1, matrix products, shards(): jnp.einsum('efc,eskf->csek', w_down, hidden, preferred_element_type=jnp.f...  12.3 us
  transfers between devices with their start and end apart: 3, of which 3 were waited for; matrix products, arithmetic and copies ran while one was open for 0% of the time, Pallas kernels for 0%

commit v1 on v0

v1 whole, which is shorter than its diff:
```python
import functools

import jax
import jax.numpy as jnp
from jax import lax
from jax.experimental import pallas as pl
from jax.experimental.pallas import tpu as pltpu
from jax.sharding import PartitionSpec as P

CAP = 21
PACK = 32
LANES = 128
SIDE = 4
F32 = jnp.float32
BF16 = jnp.bfloat16


def mm(a, b):
    return jnp.dot(a, b, preferred_element_type=F32)


def mm_t(a, b):
    return lax.dot_general(a, b, (((0,), (0,)), ((), ())), preferred_element_type=F32)


def layer(
    experts, tok_ref, ids_ref, rw_ref, wup_ref, wdn_ref, out_ref,
    sbuf, ag, wu, wraw, wd, acc, hp, a_up, a_dn, b_up, b_dn, ra_up, ra_dn, rb_up, rb_dn,
    keep_up, keep_dn, own, zs, zr, fbuf, rbuf,
    wsem, d_s, d_r, z_s, z_r, y_s, y_r, r_s, r_r, zz_s, zz_r, t_s, t_r,
):
    topk = ids_ref.shape[1]
    tokens = tok_ref.shape[0]
    rows = experts * PACK
    half = rows // 2
    width = wup_ref.shape[2]
    e = lax.axis_index("expert")
    s = lax.axis_index("seg")
    zl, y = s // SIDE, s % SIDE
    up = (y + 1) % SIDE
    down = (y + SIDE - 1) % SIDE
    far = (y + 2) % SIDE
    zpeer = [zl, zl + 1 - 2 * (zl % 2), (zl + 2) % SIDE, SIDE - 1 - zl]
    seg_up, seg_down = zl * SIDE + up, zl * SIDE + down

    barrier = pltpu.get_barrier_semaphore()

    def greet(i, c):
        pl.semaphore_signal(barrier, inc=1, device_id={"expert": (e + i) % experts})
        return c

    lax.fori_loop(1, experts, greet, 0)
    for to in (seg_up, seg_down, *[zpeer[j] * SIDE + y for j in range(1, SIDE)]):
        pl.semaphore_signal(barrier, inc=1, device_id={"seg": to})

    loads = [
        pltpu.make_async_copy(wup_ref.at[:, 0:128, :], wu.at[:, :, 0:width], wsem.at[0]),
        pltpu.make_async_copy(wup_ref.at[:, 128:192, :], wu.at[:, 0:64, width : 2 * width], wsem.at[1]),
        pltpu.make_async_copy(wup_ref.at[:, 128:192, :], wu.at[:, 64:128, 2 * width : 3 * width], wsem.at[2]),
        pltpu.make_async_copy(wdn_ref, wraw, wsem.at[3]),
    ]
    for c in loads:
        c.start()

    lane = lax.broadcasted_iota(jnp.int32, (tokens, rows), 1)
    lane_e, lane_r = lane // PACK, lane % PACK
    ids = ids_ref[...]
    rw = rw_ref[...]
    norm = rw / jnp.sum(rw, axis=1, keepdims=True)
    weight = jnp.zeros((tokens, rows), F32)
    named = jnp.zeros((tokens, rows), F32)
    for k in range(topk):
        hit = ids[:, k : k + 1] == lane_e
        named = jnp.where(hit, 1.0, named)
        weight = jnp.where(hit, norm[:, k : k + 1], weight)
    earlier = lax.broadcasted_iota(jnp.int32, (tokens, tokens), 1) < lax.broadcasted_iota(
        jnp.int32, (tokens, tokens), 0
    )
    slot = mm(jnp.where(earlier, 1.0, 0.0).astype(BF16), named.astype(BF16)).astype(jnp.int32)
    main = lane_r < CAP
    place = jnp.concatenate(
        [
            jnp.where(main & (slot == lane_r), named, 0.0),
            jnp.where(~main & (slot == lane_r - CAP), named, 0.0),
            jnp.where(~main & (slot == lane_r - 10), named, 0.0),
        ],
        axis=0,
    )
    tok = tok_ref[...]
    rest = tok[:, 128:192].astype(F32)
    blank = jnp.zeros((tokens, 64), F32)
    source = jnp.concatenate(
        [
            tok[:, 0:128],
            jnp.concatenate([rest, blank], axis=1).astype(BF16),
            jnp.concatenate([blank, rest], axis=1).astype(BF16),
        ],
        axis=0,
    )
    sbuf[...] = mm_t(place.astype(BF16), source).astype(BF16)

    pl.semaphore_wait(barrier, experts - 1 + SIDE + 1)

    def dispatch(i):
        to = (e + i) % experts
        return pltpu.make_async_remote_copy(
            src_ref=sbuf.at[pl.ds(to * PACK, PACK)],
            dst_ref=ag.at[s, pl.ds(e * PACK, PACK)],
            send_sem=d_s.at[i],
            recv_sem=d_r.at[i],
            device_id={"expert": to},
        )

    def start_dispatch(i, c):
        dispatch(i).start()
        return c

    lax.fori_loop(1, experts, start_dispatch, 0)
    ag[s, pl.ds(e * PACK, PACK), :] = sbuf[pl.ds(e * PACK, PACK), :]

    wu[:, 64:128, width : 2 * width] = jnp.zeros((wu.shape[0], 64, width), BF16)
    wu[:, 0:64, 2 * width : 3 * width] = jnp.zeros((wu.shape[0], 64, width), BF16)
    loads[3].wait()
    left = lax.broadcasted_iota(jnp.int32, (width, LANES), 1) < 64

    def pad_down(i, c):
        z, q = i // 2, i % 2
        base = pl.multiple_of(i * 384, 128)
        a = wraw[:, pl.ds(base, 128)]
        b = wraw[:, pl.ds(base + 128, 128)].astype(F32)
        g = wraw[:, pl.ds(base + 256, 128)].astype(F32)
        b_turn, g_turn = pltpu.roll(b, 64, 1), pltpu.roll(g, 64, 1)
        to0 = pl.multiple_of((2 * q + 6 - y) % SIDE * LANES, LANES)
        to1 = pl.multiple_of((2 * q + 7 - y) % SIDE * LANES, LANES)
        wd[z, 0:width, pl.ds(to0, LANES)] = a
        wd[z, width : 2 * width, pl.ds(to0, LANES)] = jnp.where(left, b, 0.0).astype(BF16)
        wd[z, 2 * width : 3 * width, pl.ds(to0, LANES)] = jnp.where(left, 0.0, b_turn).astype(BF16)
        wd[z, 0:width, pl.ds(to1, LANES)] = jnp.where(left, b_turn, g_turn).astype(BF16)
        wd[z, width : 2 * width, pl.ds(to1, LANES)] = jnp.where(left, g_turn, 0.0).astype(BF16)
        wd[z, 2 * width : 3 * width, pl.ds(to1, LANES)] = jnp.where(left, 0.0, g).astype(BF16)
        return c

    lax.fori_loop(0, 2 * SIDE, pad_down, 0)
    for c in loads[:3]:
        c.wait()

    def wait_dispatch(i, c):
        dispatch(i).wait_recv()
        return c

    lax.fori_loop(1, experts, wait_dispatch, 0)

    def zcopy(j):
        return pltpu.make_async_remote_copy(
            src_ref=ag.at[s],
            dst_ref=ag.at[s],
            send_sem=z_s.at[j],
            recv_sem=z_r.at[j],
            device_id={"seg": zpeer[j] * SIDE + y},
        )

    def z_arrival(j):
        g = zpeer[j] * SIDE + y
        return pltpu.make_async_remote_copy(
            src_ref=ag.at[g], dst_ref=ag.at[g], send_sem=z_s.at[j], recv_sem=z_r.at[j], device_id={"seg": g}
        )

    lo, hi = pl.ds(0, half), pl.ds(half, half)

    def ycopy(j, line, col, part, to):
        g = zpeer[j] * SIDE + col
        return pltpu.make_async_remote_copy(
            src_ref=ag.at[g, part],
            dst_ref=ag.at[g, part],
            send_sem=y_s.at[j, line],
            recv_sem=y_r.at[j, line],
            device_id={"seg": to},
        )

    def y_send(j):
        for c in (
            ycopy(j, 0, y, lo, seg_up),
            ycopy(j, 1, y, hi, seg_down),
            ycopy(j, 2, y, hi, seg_up),
            ycopy(j, 3, y, lo, seg_down),
        ):
            c.start()

    def y_pass(j):
        ycopy(j, 0, down, lo, seg_up).wait_recv()
        ycopy(j, 4, down, lo, seg_up).start()
        ycopy(j, 1, up, hi, seg_down).wait_recv()
        ycopy(j, 5, up, hi, seg_down).start()

    def up_part(j, first):
        ycopy(j, 2, down, hi, seg_up).wait_recv()
        ycopy(j, 3, up, lo, seg_down).wait_recv()
        ycopy(j, 4, far, lo, seg_up).wait_recv()
        ycopy(j, 5, far, hi, seg_down).wait_recv()
        g = zpeer[j] * SIDE
        x = jnp.concatenate([ag[g + i] for i in range(SIDE)], axis=1)
        w = wu[pl.ds(g, SIDE)].reshape(SIDE * LANES, 3 * width)
        if first:
            acc[...] = mm(x, w)
        else:
            acc[...] += mm(x, w)

    for j in range(1, SIDE):
        zcopy(j).start()
    y_send(0)
    for j in range(1, SIDE):
        z_arrival(j).wait_recv()
        y_send(j)
        y_pass(j - 1)
        if j > 1:
            up_part(j - 2, j == 2)
    y_pass(SIDE - 1)
    up_part(SIDE - 2, False)
    up_part(SIDE - 1, False)

    r = lax.broadcasted_iota(jnp.int32, (rows, width), 0) % PACK
    spread = jnp.where(
        r < 11,
        pltpu.roll(acc[:, width : 2 * width], rows - 21, 0),
        pltpu.roll(acc[:, 2 * width : 3 * width], rows - 10, 0),
    )
    v = acc[:, 0:width] + spread
    h = jnp.where(r < CAP, v / (1.0 + jnp.exp(-v)), 0.0)
    hp[:, 0:width] = h.astype(BF16)
    hp[:, width : 2 * width] = jnp.where(r < CAP, 0.0, pltpu.roll(h, 21, 0)).astype(BF16)
    hp[:, 2 * width : 3 * width] = jnp.where(r < CAP, 0.0, pltpu.roll(h, 10, 0)).astype(BF16)

    def rcopy(j, line, src, dst, to):
        return pltpu.make_async_remote_copy(
            src_ref=src,
            dst_ref=dst,
            send_sem=r_s.at[j, line],
            recv_sem=r_r.at[j, line],
            device_id={"seg": to},
        )

    def line(j, n):
        return (
            lambda: rcopy(j, 0, a_up.at[j], ra_up.at[j], seg_up),
            lambda: rcopy(j, 1, a_dn.at[j], ra_dn.at[j], seg_down),
            lambda: rcopy(j, 2, b_up.at[j, hi], rb_up.at[j, hi], seg_up),
            lambda: rcopy(j, 3, b_dn.at[j, lo], rb_dn.at[j, lo], seg_down),
            lambda: rcopy(j, 4, b_up.at[j, lo], rb_up.at[j, lo], seg_up),
            lambda: rcopy(j, 5, b_dn.at[j, hi], rb_dn.at[j, hi], seg_down),
        )[n]()

    def down_first(j):
        part = mm(hp[...], wd[zpeer[j]])
        a_up[j] = part[0:half, 0:128].astype(BF16)
        a_dn[j] = part[half:rows, 0:128].astype(BF16)
        line(j, 0).start()
        line(j, 1).start()
        b_up[j, half:rows] = part[half:rows, 384:512].astype(BF16)
        b_dn[j, 0:half] = part[0:half, 128:256].astype(BF16)
        line(j, 2).start()
        line(j, 3).start()
        keep_up[j] = part[0:half, 384:512]
        keep_dn[j] = part[half:rows, 128:256]
        own[j] = part[:, 256:384]

    def down_second(j):
        line(j, 0).wait_recv()
        b_up[j, 0:half] = (keep_up[j] + ra_up[j].astype(F32)).astype(BF16)
        line(j, 4).start()
        line(j, 1).wait_recv()
        b_dn[j, half:rows] = (keep_dn[j] + ra_dn[j].astype(F32)).astype(BF16)
        line(j, 5).start()

    def zsum(j):
        return pltpu.make_async_remote_copy(
            src_ref=zs.at[j],
            dst_ref=zr.at[j],
            send_sem=zz_s.at[j],
            recv_sem=zz_r.at[j],
            device_id={"seg": zpeer[j] * SIDE + y},
        )

    def down_third(j):
        for n in range(2, 6):
            line(j, n).wait_recv()
        total = own[j] + rb_up[j].astype(F32) + rb_dn[j].astype(F32)
        if j:
            zs[j] = total.astype(BF16)
            zsum(j).start()
        else:
            own[j] = total

    down_first(1)
    down_first(2)
    down_second(1)
    down_first(3)
    down_second(2)
    down_third(1)
    down_first(0)
    down_second(3)
    down_third(2)
    down_second(0)
    down_third(3)
    down_third(0)
    total = own[0]
    for j in range(1, SIDE):
        zsum(j).wait_recv()
        total += zr[j].astype(F32)
    fbuf[...] = total.astype(BF16)

    def back(i):
        to = (e + i) % experts
        return pltpu.make_async_remote_copy(
            src_ref=fbuf.at[pl.ds(to * PACK, PACK)],
            dst_ref=rbuf.at[pl.ds(e * PACK, PACK)],
            send_sem=t_s.at[i],
            recv_sem=t_r.at[i],
            device_id={"expert": to},
        )

    def start_back(i, c):
        back(i).start()
        return c

    lax.fori_loop(1, experts, start_back, 0)
    rbuf[pl.ds(e * PACK, PACK), :] = fbuf[pl.ds(e * PACK, PACK), :]
    scaled = place * jnp.concatenate([weight] * 3, axis=0)
    big = scaled.astype(BF16)
    small = (scaled - big.astype(F32)).astype(BF16)

    for j in range(SIDE):
        if j:
            zcopy(j).wait_send()
            zsum(j).wait_send()
        ycopy(j, 0, y, lo, seg_up).wait_send()
        ycopy(j, 1, y, hi, seg_down).wait_send()
        ycopy(j, 2, y, hi, seg_up).wait_send()
        ycopy(j, 3, y, lo, seg_down).wait_send()
        ycopy(j, 4, down, lo, seg_up).wait_send()
        ycopy(j, 5, up, hi, seg_down).wait_send()
        for n in range(6):
            line(j, n).wait_send()

    def wait_sent(i, c):
        dispatch(i).wait_send()
        back(i).wait_send()
        return c

    lax.fori_loop(1, experts, wait_sent, 0)

    def wait_back(i, c):
        back(i).wait_recv()
        return c

    lax.fori_loop(1, experts, wait_back, 0)
    got = rbuf[...]
    mixed = mm(big, got) + mm(small, got)
    out_ref[:, 0:128] = mixed[0:tokens].astype(BF16)
    tail = mixed[tokens : 2 * tokens, 0:64] + mixed[2 * tokens : 3 * tokens, 64:128]
    out_ref[:, 128:192] = tail.astype(BF16)


def shards(experts, tokens, expert_ids, route_weight, w_up, w_down):
    segs = SIDE * SIDE
    rows = experts * PACK
    half = rows // 2
    width = w_up.shape[2]
    block = tokens.shape[1]
    vm = pltpu.VMEM
    dma = pltpu.SemaphoreType.DMA
    return pl.pallas_call(
        functools.partial(layer, experts),
        out_shape=jax.ShapeDtypeStruct(tokens.shape, BF16),
        in_specs=[pl.BlockSpec(memory_space=vm)] * 3 + [pl.BlockSpec(memory_space=pl.ANY)] * 2,
        out_specs=pl.BlockSpec(memory_space=vm),
        scratch_shapes=[
            vm((rows, LANES), BF16),
            vm((segs, rows, LANES), BF16),
            vm((segs, LANES, 3 * width), BF16),
            vm((width, segs * block), BF16),
            vm((SIDE, 3 * width, SIDE * LANES), BF16),
            vm((rows, 3 * width), F32),
            vm((rows, 3 * width), BF16),
            vm((SIDE, half, LANES), BF16),
            vm((SIDE, half, LANES), BF16),
            vm((SIDE, rows, LANES), BF16),
            vm((SIDE, rows, LANES), BF16),
            vm((SIDE, half, LANES), BF16),
            vm((SIDE, half, LANES), BF16),
            vm((SIDE, rows, LANES), BF16),
            vm((SIDE, rows, LANES), BF16),
            vm((SIDE, half, LANES), F32),
            vm((SIDE, half, LANES), F32),
            vm((SIDE, rows, LANES), F32),
            vm((SIDE, rows, LANES), BF16),
            vm((SIDE, rows, LANES), BF16),
            vm((rows, LANES), BF16),
            vm((rows, LANES), BF16),
            dma((4,)),
            dma((experts,)),
            dma((experts,)),
            dma((SIDE,)),
            dma((SIDE,)),
            dma((SIDE, 6)),
            dma((SIDE, 6)),
            dma((SIDE, 6)),
            dma((SIDE, 6)),
            dma((SIDE,)),
            dma((SIDE,)),
            dma((experts,)),
            dma((experts,)),
        ],
        compiler_params=pltpu.CompilerParams(
            collective_id=0, has_side_effects=True, vmem_limit_bytes=56 * 2**20
        ),
    )(
        tokens,
        expert_ids,
        route_weight,
        w_up.reshape(segs, block, width),
        w_down.reshape(width, segs * block),
    )


def solution(mesh):
    placed = (
        P(("dp", "expert"), "seg"),
        P(("dp", "expert"), None),
        P(("dp", "expert"), None),
        P("expert", None, "seg"),
        P("expert", "seg", None),
    )
    return jax.shard_map(
        functools.partial(shards, mesh.shape["expert"]),
        mesh=mesh,
        in_specs=placed,
        out_specs=P(("dp", "expert"), "seg"),
        check_vma=False,
    )
```

time: 355 us -> 92.5 us (0.26)
  the two profiles are of different devices: /device:TPU:2 before, /device:TPU:72 now
where the time goes in v1:
time: 92.5 us; the launch traced here: 92.3 us
  Pallas kernels  88.1 us (95%)
  local copies, waits for them, and re-layouts  4.13 us (4%)
    pallas_call x1, Pallas kernels, shards(): pl.pallas_call(functools.partial(layer, experts), out_shape=jax.ShapeDtyp...  88.1 us
    unnamed x3, local copies, waits for them, and re-layouts  4.13 us

profile of v1, /device:TPU:72, one launch (start us, length us, event | category | flops | bytes accessed | tf_op | source)
XLA Modules:
  0.0 92.3 jit_solution(12327973320123216113)
XLA Ops:
  0.0 1.4 %copy.6.ids_ref = s32[64,4]{1,0:T(8,128)} copy(s32[64,4]{0,1:T(4,128)} %param.6) | data formatting | bytes 2048 | tf_op args[1]
  1.4 1.4 %copy.7.rw_ref = f32[64,4]{1,0:T(8,128)} copy(f32[64,4]{0,1:T(4,128)} %param.7) | data formatting | bytes 2048 | tf_op args[2]
  2.8 88.1 %shard_map.55 = bf16[64,192]{1,0:T(8,128)(2,1)} custom-call(bf16[64,192]{1,0:T(8,128)(2,1)} %tok_ref.1, s32[64,4]{1,0:T(8,128)} %copy.6.ids_ref, f32[64,4]{1,0:T(8,128)} %copy.7.rw_ref, bf16[16,192,384]{2,1,0:T(8,128)(2,1)} %bitcast.2, bf16[384,3072]{1,0:T(8,128)(2,1)} %bitcast.3), custom_call_target="tpu_custom_call" | custom-call | tf_op jit(solution)/shard_map/pallas_call | solution.py:371
  90.9 1.4 %copy.9 = bf16[64,192]{1,0:T(8,128)(2,1)} copy(bf16[64,192]{1,0:T(8,128)(2,1)} %shard_map.55) | data formatting | bytes 49152

commit v2 on v0

v2 whole, which is shorter than its diff:
```python
import functools

import jax
import jax.numpy as jnp
from jax import lax
from jax.experimental import pallas as pl
from jax.experimental.pallas import tpu as pltpu
from jax.sharding import PartitionSpec as P

CAP = 21
PACK = 32
LANES = 128
SIDE = 4
OFF = (0, 1, 3, 2)
LAG2, LAG3, LAG4 = 3, 6, 3
F32 = jnp.float32
BF16 = jnp.bfloat16


def mm(a, b):
    return jnp.dot(a, b, preferred_element_type=F32)


def mm_t(a, b):
    return lax.dot_general(a, b, (((0,), (0,)), ((), ())), preferred_element_type=F32)


def layer(
    experts, tok_ref, ids_ref, rw_ref, wup_ref, wdn_ref, out_ref,
    sbuf, mid, ag, wu, wraw, wd, hp, place, a_up, a_dn, b_up, b_dn, ra_up, ra_dn, rb_up, rb_dn,
    keep_up, keep_dn, own, zs, zr, fb, rb1, rb2,
    wsem, dx_s, dx_r, dz_s, dz_r, z_s, z_r, y_s, y_r, r_s, r_r, zz_s, zz_r, th_s, th_r, tx_s, tx_r,
):
    topk = ids_ref.shape[0]
    tokens = tok_ref.shape[0]
    xs = experts // SIDE
    chunk = xs * PACK
    half = chunk // 2
    rows = SIDE * chunk
    width = wup_ref.shape[2]
    e = lax.axis_index("expert")
    s = lax.axis_index("seg")
    zh, x = e // xs, e % xs
    zl, y = s // SIDE, s % SIDE
    up = (y + 1) % SIDE
    down = (y + SIDE - 1) % SIDE
    far = (y + 2) % SIDE
    zpeer = [zl, zl + 1 - 2 * (zl % 2), (zl + 2) % SIDE, SIDE - 1 - zl]
    seg_up, seg_down = zl * SIDE + up, zl * SIDE + down

    def at_zh(off):
        return {"expert": (zh + SIDE + off) % SIDE * xs + x}

    def at_x(i):
        return {"expert": zh * xs + (x + i) % xs}

    barrier = pltpu.get_barrier_semaphore()
    near = [at_x(i) for i in range(1, xs)] + [at_zh(1), at_zh(-1)]
    near += [{"seg": seg_up}, {"seg": seg_down}]
    near += [{"seg": zpeer[j] * SIDE + y} for j in range(1, SIDE)]
    for to in near:
        pl.semaphore_signal(barrier, inc=1, device_id=to)

    loads = [
        pltpu.make_async_copy(wup_ref.at[:, 0:128, :], wu.at[:, :, 0:width], wsem.at[0]),
        pltpu.make_async_copy(wup_ref.at[:, 128:192, :], wu.at[:, 0:64, width : 2 * width], wsem.at[1]),
        pltpu.make_async_copy(wup_ref.at[:, 128:192, :], wu.at[:, 64:128, 2 * width : 3 * width], wsem.at[2]),
        pltpu.make_async_copy(wdn_ref, wraw, wsem.at[3]),
    ]
    for c in loads:
        c.start()

    table = jnp.concatenate([ids_ref[...].astype(F32), rw_ref[...]], axis=0).T
    ids, rw = table[:, 0:topk], table[:, topk : 2 * topk]
    norm = rw / jnp.sum(rw, axis=1, keepdims=True)
    lane = lax.broadcasted_iota(jnp.int32, (tokens, rows), 1)
    lane_c, lane_x, lane_r = lane // chunk, lane % chunk // PACK, lane % PACK
    lane_off = jnp.where(lane_c == 0, 0, jnp.where(lane_c == 1, 1, 5 - lane_c))
    lane_e = ((zh + SIDE - lane_off) % SIDE * xs + lane_x).astype(F32)
    weight = jnp.zeros((tokens, rows), F32)
    named = jnp.zeros((tokens, rows), F32)
    for k in range(topk):
        hit = ids[:, k : k + 1] == lane_e
        named = jnp.where(hit, 1.0, named)
        weight = jnp.where(hit, norm[:, k : k + 1], weight)
    earlier = lax.broadcasted_iota(jnp.int32, (tokens, tokens), 1) < lax.broadcasted_iota(
        jnp.int32, (tokens, tokens), 0
    )
    slot = mm(jnp.where(earlier, 1.0, 0.0).astype(BF16), named.astype(BF16)).astype(jnp.int32)
    main = lane_r < CAP
    puts = (main & (slot == lane_r), ~main & (slot == lane_r - CAP), ~main & (slot == lane_r - 10))
    tok = tok_ref[...]
    rest = tok[:, 128:192].astype(F32)
    blank = jnp.zeros((tokens, 64), F32)
    source = jnp.concatenate(
        [
            tok[:, 0:128],
            jnp.concatenate([rest, blank], axis=1).astype(BF16),
            jnp.concatenate([blank, rest], axis=1).astype(BF16),
        ],
        axis=0,
    )
    onehot = jnp.concatenate([jnp.where(p, named, 0.0) for p in puts], axis=0)
    sbuf[...] = mm_t(onehot.astype(BF16), source).astype(BF16).reshape(SIDE, chunk, LANES)

    pl.semaphore_wait(barrier, len(near))

    def first_x(i):
        to = (x + i) % xs
        return pltpu.make_async_remote_copy(
            src_ref=sbuf.at[0, pl.ds(to * PACK, PACK)],
            dst_ref=ag.at[0, s, pl.ds(x * PACK, PACK)],
            send_sem=dx_s.at[0, i],
            recv_sem=dx_r.at[0, i],
            device_id=at_x(i),
        )

    def other_x(i):
        to = (x + i) % xs
        return pltpu.make_async_remote_copy(
            src_ref=sbuf.at[pl.ds(1, SIDE - 1), pl.ds(to * PACK, PACK)],
            dst_ref=mid.at[:, pl.ds(x * PACK, PACK)],
            send_sem=dx_s.at[1, i],
            recv_sem=dx_r.at[1, i],
            device_id=at_x(i),
        )

    def across(c):
        return pltpu.make_async_remote_copy(
            src_ref=mid.at[c - 1],
            dst_ref=ag.at[c, s],
            send_sem=dz_s.at[c],
            recv_sem=dz_r.at[c],
            device_id=at_zh(-OFF[c]),
        )

    for i in range(1, xs):
        first_x(i).start()
    for i in range(1, xs):
        other_x(i).start()
    mine = pl.ds(x * PACK, PACK)
    ag[0, s, mine, :] = sbuf[0, mine, :]
    for c in range(1, SIDE):
        mid[c - 1, mine, :] = sbuf[c, mine, :]

    def zcopy(c, j):
        return pltpu.make_async_remote_copy(
            src_ref=ag.at[c, s],
            dst_ref=ag.at[c, s],
            send_sem=z_s.at[c, j],
            recv_sem=z_r.at[c, j],
            device_id={"seg": zpeer[j] * SIDE + y},
        )

    def z_arrival(c, j):
        g = zpeer[j] * SIDE + y
        return pltpu.make_async_remote_copy(
            src_ref=ag.at[c, g],
            dst_ref=ag.at[c, g],
            send_sem=z_s.at[c, j],
            recv_sem=z_r.at[c, j],
            device_id={"seg": g},
        )

    def ycopy(c, j, line):
        col, part, to = (
            (y, pl.ds(0, chunk), seg_up),
            (y, pl.ds(0, chunk), seg_down),
            (down, pl.ds(0, half), seg_up),
            (up, pl.ds(half, half), seg_down),
        )[line]
        g = zpeer[j] * SIDE + col
        return pltpu.make_async_remote_copy(
            src_ref=ag.at[c, g, part],
            dst_ref=ag.at[c, g, part],
            send_sem=y_s.at[c, j, line],
            recv_sem=y_r.at[c, j, line],
            device_id={"seg": to},
        )

    def y_arrival(c, j, line):
        col, part = (
            (down, pl.ds(0, chunk)),
            (up, pl.ds(0, chunk)),
            (far, pl.ds(0, half)),
            (far, pl.ds(half, half)),
        )[line]
        g = zpeer[j] * SIDE + col
        return pltpu.make_async_remote_copy(
            src_ref=ag.at[c, g, part],
            dst_ref=ag.at[c, g, part],
            send_sem=y_s.at[c, j, line],
            recv_sem=y_r.at[c, j, line],
            device_id={"seg": seg_up},
        )

    def y_send(c, j):
        ycopy(c, j, 0).start()
        ycopy(c, j, 1).start()

    def own_out(c):
        for j in range(1, SIDE):
            zcopy(c, j).start()
        y_send(c, 0)

    def z_out(c):
        for j in range(1, SIDE):
            z_arrival(c, j).wait_recv()
            y_send(c, j)

    def y_pass(c):
        for j in range(SIDE):
            y_arrival(c, j, 0).wait_recv()
            ycopy(c, j, 2).start()
            y_arrival(c, j, 1).wait_recv()
            ycopy(c, j, 3).start()

    r = lax.broadcasted_iota(jnp.int32, (chunk, width), 0) % PACK

    def up_part(c):
        for j in range(SIDE):
            y_arrival(c, j, 2).wait_recv()
            y_arrival(c, j, 3).wait_recv()
        lhs = jnp.concatenate([ag[c, g] for g in range(SIDE * SIDE)], axis=1)
        u = mm(lhs, wu[...].reshape(SIDE * SIDE * LANES, 3 * width))
        v = u[:, 0:width] + jnp.where(
            r < 11,
            pltpu.roll(u[:, width : 2 * width], chunk - 21, 0),
            pltpu.roll(u[:, 2 * width : 3 * width], chunk - 10, 0),
        )
        h = jnp.where(r < CAP, v / (1.0 + jnp.exp(-v)), 0.0)
        hp[c, :, 0:width] = h.astype(BF16)
        hp[c, :, width : 2 * width] = jnp.where(r < CAP, 0.0, pltpu.roll(h, 21, 0)).astype(BF16)
        hp[c, :, 2 * width : 3 * width] = jnp.where(r < CAP, 0.0, pltpu.roll(h, 10, 0)).astype(BF16)

    left = lax.broadcasted_iota(jnp.int32, (width, LANES), 1) < 64

    def pad_down(i, c):
        z, q = i // 2, i % 2
        base = pl.multiple_of(i * 384, 128)
        a = wraw[:, pl.ds(base, 128)]
        b = wraw[:, pl.ds(base + 128, 128)].astype(F32)
        g = wraw[:, pl.ds(base + 256, 128)].astype(F32)
        b_turn, g_turn = pltpu.roll(b, 64, 1), pltpu.roll(g, 64, 1)
        to0 = pl.multiple_of((2 * q + 6 - y) % SIDE * LANES, LANES)
        to1 = pl.multiple_of((2 * q + 7 - y) % SIDE * LANES, LANES)
        wd[z, 0:width, pl.ds(to0, LANES)] = a
        wd[z, width : 2 * width, pl.ds(to0, LANES)] = jnp.where(left, b, 0.0).astype(BF16)
        wd[z, 2 * width : 3 * width, pl.ds(to0, LANES)] = jnp.where(left, 0.0, b_turn).astype(BF16)
        wd[z, 0:width, pl.ds(to1, LANES)] = jnp.where(left, b_turn, g_turn).astype(BF16)
        wd[z, width : 2 * width, pl.ds(to1, LANES)] = jnp.where(left, g_turn, 0.0).astype(BF16)
        wd[z, 2 * width : 3 * width, pl.ds(to1, LANES)] = jnp.where(left, 0.0, g).astype(BF16)
        return c

    for i in range(1, xs):
        first_x(i).wait_recv()
    own_out(0)
    for i in range(1, xs):
        other_x(i).wait_recv()
    across(1).start()
    across(2).start()
    wu[:, 64:128, width : 2 * width] = jnp.zeros((wu.shape[0], 64, width), BF16)
    wu[:, 0:64, 2 * width : 3 * width] = jnp.zeros((wu.shape[0], 64, width), BF16)
    z_out(0)
    across(1).wait_recv()
    across(3).start()
    own_out(1)
    y_pass(0)
    loads[3].wait()
    lax.fori_loop(0, SIDE, pad_down, 0)
    z_out(1)
    across(2).wait_recv()
    own_out(2)
    y_pass(1)
    for c in loads[:3]:
        c.wait()
    up_part(0)
    z_out(2)
    across(3).wait_recv()
    own_out(3)
    y_pass(2)
    lax.fori_loop(SIDE, 2 * SIDE, pad_down, 0)
    up_part(1)
    z_out(3)
    y_pass(3)
    scaled = jnp.concatenate([jnp.where(p, weight, 0.0) for p in puts], axis=0)
    place[0] = scaled.astype(BF16)
    place[1] = (scaled - scaled.astype(BF16).astype(F32)).astype(BF16)
    up_part(2)
    up_part(3)

    def line(c, j, n):
        src, dst, to = (
            (a_up, ra_up, seg_up),
            (a_dn, ra_dn, seg_down),
            (b_up, rb_up, seg_up),
            (b_dn, rb_dn, seg_down),
        )[n]
        return pltpu.make_async_remote_copy(
            src_ref=src.at[c, j],
            dst_ref=dst.at[c, j],
            send_sem=r_s.at[c, j, n],
            recv_sem=r_r.at[c, j, n],
            device_id={"seg": to},
        )

    def down_first(c, j):
        part = mm(hp[c], wd[zpeer[j]])
        a_up[c, j] = part[0:half, 0:128].astype(BF16)
        a_dn[c, j] = part[half:chunk, 0:128].astype(BF16)
        line(c, j, 0).start()
        line(c, j, 1).start()
        b_up[c, j, half:chunk] = part[half:chunk, 384:512].astype(BF16)
        b_dn[c, j, 0:half] = part[0:half, 128:256].astype(BF16)
        keep_up[c, j] = part[0:half, 384:512]
        keep_dn[c, j] = part[half:chunk, 128:256]
        own[c, j] = part[:, 256:384]

    def down_second(c, j):
        line(c, j, 0).wait_recv()
        b_up[c, j, 0:half] = (keep_up[c, j] + ra_up[c, j].astype(F32)).astype(BF16)
        line(c, j, 2).start()
        line(c, j, 1).wait_recv()
        b_dn[c, j, half:chunk] = (keep_dn[c, j] + ra_dn[c, j].astype(F32)).astype(BF16)
        line(c, j, 3).start()

    def zsum(c, j):
        return pltpu.make_async_remote_copy(
            src_ref=zs.at[c, j],
            dst_ref=zr.at[c, j],
            send_sem=zz_s.at[c, j],
            recv_sem=zz_r.at[c, j],
            device_id={"seg": zpeer[j] * SIDE + y},
        )

    def down_third(c, j):
        line(c, j, 2).wait_recv()
        line(c, j, 3).wait_recv()
        total = own[c, j] + rb_up[c, j].astype(F32) + rb_dn[c, j].astype(F32)
        if j:
            zs[c, j] = total.astype(BF16)
            zsum(c, j).start()
        else:
            own[c, j] = total

    def home(c):
        return pltpu.make_async_remote_copy(
            src_ref=fb.at[c],
            dst_ref=rb1.at[c],
            send_sem=th_s.at[c],
            recv_sem=th_r.at[c],
            device_id=at_zh(OFF[c]),
        )

    def finish(c):
        total = own[c, 0]
        for j in range(1, SIDE):
            zsum(c, j).wait_recv()
            total += zr[c, j].astype(F32)
        if c:
            fb[c] = total.astype(BF16)
            home(c).start()
        else:
            rb1[c] = total.astype(BF16)

    def share(c, i):
        to = (x + i) % xs
        return pltpu.make_async_remote_copy(
            src_ref=rb1.at[c, pl.ds(to * PACK, PACK)],
            dst_ref=rb2.at[c, pl.ds(x * PACK, PACK)],
            send_sem=tx_s.at[c, i],
            recv_sem=tx_r.at[c, i],
            device_id=at_x(i),
        )

    def spread(c):
        if c:
            home(c).wait_recv()
        for i in range(1, xs):
            share(c, i).start()
        rb2[c, mine, :] = rb1[c, mine, :]

    order = [(c, j) for c in (3, 1, 2, 0) for j in (1, 2, 3, 0)]
    done = {3: 0, 1: 0, 2: 0, 0: 0}
    for n in range(len(order) + LAG3 + LAG4):
        if n < len(order):
            down_first(*order[n])
        if 0 <= n - LAG2 < len(order):
            down_second(*order[n - LAG2])
        if 0 <= n - LAG3 < len(order):
            down_third(*order[n - LAG3])
        m = n - LAG3 - LAG4
        if 0 <= m < len(order) and m % SIDE == SIDE - 1 and order[m][0]:
            finish(order[m][0])
    spread(3)
    spread(1)
    finish(0)
    spread(0)
    spread(2)

    for i in range(1, xs):
        first_x(i).wait_send()
        other_x(i).wait_send()
    for c in range(SIDE):
        if c:
            across(c).wait_send()
            home(c).wait_send()
        for i in range(1, xs):
            share(c, i).wait_send()
        for j in range(SIDE):
            if j:
                zcopy(c, j).wait_send()
                zsum(c, j).wait_send()
            for n in range(4):
                ycopy(c, j, n).wait_send()
                line(c, j, n).wait_send()
    for c in range(SIDE):
        for i in range(1, xs):
            share(c, i).wait_recv()
    got = rb2[...].reshape(rows, LANES)
    mixed = mm(place[0], got) + mm(place[1], got)
    out_ref[:, 0:128] = mixed[0:tokens].astype(BF16)
    tail = mixed[tokens : 2 * tokens, 0:64] + mixed[2 * tokens : 3 * tokens, 64:128]
    out_ref[:, 128:192] = tail.astype(BF16)


def shards(experts, tokens, expert_ids, route_weight, w_up, w_down):
    segs = SIDE * SIDE
    xs = experts // SIDE
    chunk = xs * PACK
    half = chunk // 2
    width = w_up.shape[2]
    count, block = tokens.shape
    vm = pltpu.VMEM
    dma = pltpu.SemaphoreType.DMA
    each = (SIDE, SIDE)
    return pl.pallas_call(
        functools.partial(layer, experts),
        out_shape=jax.ShapeDtypeStruct(tokens.shape, BF16),
        in_specs=[pl.BlockSpec(memory_space=vm)] * 3 + [pl.BlockSpec(memory_space=pl.ANY)] * 2,
        out_specs=pl.BlockSpec(memory_space=vm),
        scratch_shapes=[
            vm((SIDE, chunk, LANES), BF16),
            vm((SIDE - 1, chunk, LANES), BF16),
            vm((SIDE, segs, chunk, LANES), BF16),
            vm((segs, LANES, 3 * width), BF16),
            vm((width, segs * block), BF16),
            vm((SIDE, 3 * width, SIDE * LANES), BF16),
            vm((SIDE, chunk, 3 * width), BF16),
            vm((2, 3 * count, SIDE * chunk), BF16),
            vm((*each, half, LANES), BF16),
            vm((*each, half, LANES), BF16),
            vm((*each, chunk, LANES), BF16),
            vm((*each, chunk, LANES), BF16),
            vm((*each, half, LANES), BF16),
            vm((*each, half, LANES), BF16),
            vm((*each, chunk, LANES), BF16),
            vm((*each, chunk, LANES), BF16),
            vm((*each, half, LANES), F32),
            vm((*each, half, LANES), F32),
            vm((*each, chunk, LANES), F32),
            vm((*each, chunk, LANES), BF16),
            vm((*each, chunk, LANES), BF16),
            vm((SIDE, chunk, LANES), BF16),
            vm((SIDE, chunk, LANES), BF16),
            vm((SIDE, chunk, LANES), BF16),
            dma((4,)),
            dma((2, xs)),
            dma((2, xs)),
            dma((SIDE,)),
            dma((SIDE,)),
            dma(each),
            dma(each),
            dma((*each, 4)),
            dma((*each, 4)),
            dma((*each, 4)),
            dma((*each, 4)),
            dma(each),
            dma(each),
            dma((SIDE,)),
            dma((SIDE,)),
            dma((SIDE, xs)),
            dma((SIDE, xs)),
        ],
        compiler_params=pltpu.CompilerParams(
            collective_id=0, has_side_effects=True, vmem_limit_bytes=56 * 2**20
        ),
    )(
        tokens,
        expert_ids.T,
        route_weight.T,
        w_up.reshape(segs, block, width),
        w_down.reshape(width, segs * block),
    )


def solution(mesh):
    placed = (
        P(("dp", "expert"), "seg"),
        P(("dp", "expert"), None),
        P(("dp", "expert"), None),
        P("expert", None, "seg"),
        P("expert", "seg", None),
    )
    return jax.shard_map(
        functools.partial(shards, mesh.shape["expert"]),
        mesh=mesh,
        in_specs=placed,
        out_specs=P(("dp", "expert"), "seg"),
        check_vma=False,
    )
```

time: 355 us -> 88.2 us (0.25)
  waiting for transfers between devices: 257 us -> 0 us
  Pallas kernels: 0 us -> 86.6 us
  blocking collectives: 35.1 us -> 0 us
  local copies, waits for them, and re-layouts: 22.5 us -> 1.38 us
  between operations: 13.5 us -> 0.01 us
  starting transfers between devices: 12.5 us -> 0 us
  matrix products: 12.3 us -> 0 us
    all_gather x1 -> x0, waiting for transfers between devices: 144 us -> none  [shards(): piece = lax.all_gather(arrived, 'seg', axis=2, tiled=True)]
    unnamed x3 -> x0, waiting for transfers between devices: 98 us -> none
    pallas_call x0 -> x1, Pallas kernels: none -> 86.6 us  [shards(): pl.pallas_call(functools.partial(layer, experts), out_shape=jax.ShapeDtyp...]
    all_to_all x1 -> x0, blocking collectives: 35.1 us -> none  [shards(): lax.all_to_all(packed, 'expert', split_axis=0, concat_axis=0, tiled=True)]
    unnamed x9 -> x1, local copies, waits for them, and re-layouts: 16.7 us -> 1.38 us
    all_to_all x1 -> x0, waiting for transfers between devices: 15.1 us -> none  [shards(): lax.all_to_all(summed, 'expert', split_axis=1, concat_axis=1, tiled=True)]
    all_to_all x1 -> x0, starting transfers between devices: 12.4 us -> none  [shards(): lax.all_to_all(summed, 'expert', split_axis=1, concat_axis=1, tiled=True)]
    dot_general x1 -> x0, matrix products: 12.3 us -> none  [shards(): jnp.einsum('efc,eskf->csek', w_down, hidden, preferred_element_type=jnp.f...]
  transfers between devices with their start and end apart: 3 -> 0, of which waited for: 3 -> 0; matrix products, arithmetic and copies ran while one was open for 0% -> 0% of each run, Pallas kernels for 0% -> 0%
where the time goes in v2:
time: 88.2 us; the launch traced here: 88 us
  Pallas kernels  86.6 us (98%)
  local copies, waits for them, and re-layouts  1.38 us (2%)
    pallas_call x1, Pallas kernels, shards(): pl.pallas_call(functools.partial(layer, experts), out_shape=jax.ShapeDtyp...  86.6 us

profile of v2, /device:TPU:2, one launch (start us, length us, event | category | flops | bytes accessed | tf_op | source)
XLA Modules:
  0.0 88.0 jit_solution(9257270432260385086)
XLA Ops:
  0.0 86.6 %shard_map.55 = bf16[64,192]{1,0:T(8,128)(2,1)} custom-call(bf16[64,192]{1,0:T(8,128)(2,1)} %tok_ref.1, s32[4,64]{1,0:T(4,128)} %bitcast.6, f32[4,64]{1,0:T(4,128)} %bitcast.7, bf16[16,192,384]{2,1,0:T(8,128)(2,1)} %bitcast.4, bf16[384,3072]{1,0:T(8,128)(2,1)} %bitcast.5), custom_call_target="tpu_custom_call" | custom-call | tf_op jit(solution)/shard_map/pallas_call | solution.py:437
  86.6 1.4 %copy.7 = bf16[64,192]{1,0:T(8,128)(2,1)} copy(bf16[64,192]{1,0:T(8,128)(2,1)} %shard_map.55) | data formatting | bytes 49152

commit v3 on v2

--- a/solution.py
+++ b/solution.py
@@ -12,7 +12,16 @@
 LANES = 128
 SIDE = 4
 OFF = (0, 1, 3, 2)
-LAG2, LAG3, LAG4 = 3, 6, 3
+GATHER_DIRECT = (0, 0, 0, 0)
+SUM_DIRECT = (0, 0, 0, 0)
+ORDER = (
+    0, 132, 136, 32, 17, 4, 8, 18, 140, 19, 33, 36, 21, 40, 34, 12,
+    35, 22, 23, 25, 37, 26, 44, 27, 48, 29, 38, 39, 30, 41, 31, 42,
+    43, 45, 52, 46, 69, 70, 47, 71, 56, 68, 85, 86, 60, 87, 77, 78,
+    84, 79, 76, 101, 73, 74, 102, 75, 72, 65, 103, 93, 66, 94, 67, 100,
+    64, 95, 92, 89, 90, 91, 88, 81, 109, 82, 116, 110, 83, 80, 111, 108,
+    105, 106, 107, 104, 97, 124, 98, 99, 96, 120, 112,
+)
 F32 = jnp.float32
 BF16 = jnp.bfloat16
 
@@ -27,9 +36,9 @@
 
 def layer(
     experts, tok_ref, ids_ref, rw_ref, wup_ref, wdn_ref, out_ref,
-    sbuf, mid, ag, wu, wraw, wd, hp, place, a_up, a_dn, b_up, b_dn, ra_up, ra_dn, rb_up, rb_dn,
-    keep_up, keep_dn, own, zs, zr, fb, rb1, rb2,
-    wsem, dx_s, dx_r, dz_s, dz_r, z_s, z_r, y_s, y_r, r_s, r_r, zz_s, zz_r, th_s, th_r, tx_s, tx_r,
+    sbuf, mid, ag, wu, wraw, wd, hp, place, a_up, a_dn, b_up, b_dn, b_far, ra_up, ra_dn, rb_up, rb_dn, rb_far,
+    keep_up, keep_dn, own, zs, zr, fb, rb2,
+    wsem, hint, dx_s, dx_r, dz_s, dz_r, z_s, z_r, y_s, y_r, r_s, r_r, zz_s, zz_r, th_s, th_r,
 ):
     topk = ids_ref.shape[0]
     tokens = tok_ref.shape[0]
@@ -46,7 +55,7 @@
     down = (y + SIDE - 1) % SIDE
     far = (y + 2) % SIDE
     zpeer = [zl, zl + 1 - 2 * (zl % 2), (zl + 2) % SIDE, SIDE - 1 - zl]
-    seg_up, seg_down = zl * SIDE + up, zl * SIDE + down
+    seg_up, seg_down, seg_far = zl * SIDE + up, zl * SIDE + down, zl * SIDE + far
 
     def at_zh(off):
         return {"expert": (zh + SIDE + off) % SIDE * xs + x}
@@ -56,7 +65,7 @@
 
     barrier = pltpu.get_barrier_semaphore()
     near = [at_x(i) for i in range(1, xs)] + [at_zh(1), at_zh(-1)]
-    near += [{"seg": seg_up}, {"seg": seg_down}]
+    near += [{"seg": seg_up}, {"seg": seg_down}, {"seg": seg_far}]
     near += [{"seg": zpeer[j] * SIDE + y} for j in range(1, SIDE)]
     for to in near:
         pl.semaphore_signal(barrier, inc=1, device_id=to)
@@ -105,43 +114,33 @@
 
     pl.semaphore_wait(barrier, len(near))
 
-    def first_x(i):
-        to = (x + i) % xs
-        return pltpu.make_async_remote_copy(
-            src_ref=sbuf.at[0, pl.ds(to * PACK, PACK)],
-            dst_ref=ag.at[0, s, pl.ds(x * PACK, PACK)],
-            send_sem=dx_s.at[0, i],
-            recv_sem=dx_r.at[0, i],
-            device_id=at_x(i),
-        )
-
-    def other_x(i):
-        to = (x + i) % xs
-        return pltpu.make_async_remote_copy(
-            src_ref=sbuf.at[pl.ds(1, SIDE - 1), pl.ds(to * PACK, PACK)],
-            dst_ref=mid.at[:, pl.ds(x * PACK, PACK)],
-            send_sem=dx_s.at[1, i],
-            recv_sem=dx_r.at[1, i],
-            device_id=at_x(i),
-        )
-
     def across(c):
         return pltpu.make_async_remote_copy(
-            src_ref=mid.at[c - 1],
-            dst_ref=ag.at[c, s],
+            src_ref=sbuf.at[c],
+            dst_ref=mid.at[c],
             send_sem=dz_s.at[c],
             recv_sem=dz_r.at[c],
             device_id=at_zh(-OFF[c]),
         )
 
-    for i in range(1, xs):
-        first_x(i).start()
-    for i in range(1, xs):
-        other_x(i).start()
+    def over_x(c, i):
+        to = (x + i) % xs
+        return pltpu.make_async_remote_copy(
+            src_ref=(mid if c else sbuf).at[c, pl.ds(to * PACK, PACK)],
+            dst_ref=ag.at[c, s, pl.ds(x * PACK, PACK)],
+            send_sem=dx_s.at[c, i],
+            recv_sem=dx_r.at[c, i],
+            device_id=at_x(i),
+        )
+
     mine = pl.ds(x * PACK, PACK)
-    ag[0, s, mine, :] = sbuf[0, mine, :]
-    for c in range(1, SIDE):
-        mid[c - 1, mine, :] = sbuf[c, mine, :]
+
+    def to_x(c):
+        if c:
+            across(c).wait_recv()
+        for i in range(1, xs):
+            over_x(c, i).start()
+        ag[c, s, mine, :] = (mid if c else sbuf)[c, mine, :]
 
     def zcopy(c, j):
         return pltpu.make_async_remote_copy(
@@ -168,6 +167,7 @@
             (y, pl.ds(0, chunk), seg_down),
             (down, pl.ds(0, half), seg_up),
             (up, pl.ds(half, half), seg_down),
+            (y, pl.ds(0, chunk), seg_far),
         )[line]
         g = zpeer[j] * SIDE + col
         return pltpu.make_async_remote_copy(
@@ -184,6 +184,7 @@
             (up, pl.ds(0, chunk)),
             (far, pl.ds(0, half)),
             (far, pl.ds(half, half)),
+            (far, pl.ds(0, chunk)),
         )[line]
         g = zpeer[j] * SIDE + col
         return pltpu.make_async_remote_copy(
@@ -197,30 +198,30 @@
     def y_send(c, j):
         ycopy(c, j, 0).start()
         ycopy(c, j, 1).start()
+        if GATHER_DIRECT[c]:
+            ycopy(c, j, 4).start()
 
     def own_out(c):
         for j in range(1, SIDE):
             zcopy(c, j).start()
         y_send(c, 0)
 
-    def z_out(c):
-        for j in range(1, SIDE):
-            z_arrival(c, j).wait_recv()
-            y_send(c, j)
-
-    def y_pass(c):
-        for j in range(SIDE):
-            y_arrival(c, j, 0).wait_recv()
-            ycopy(c, j, 2).start()
-            y_arrival(c, j, 1).wait_recv()
-            ycopy(c, j, 3).start()
+    def z_out(c, j):
+        z_arrival(c, j).wait_recv()
+        y_send(c, j)
+
+    def y_pass(c, j):
+        y_arrival(c, j, 0).wait_recv()
+        ycopy(c, j, 2).start()
+        y_arrival(c, j, 1).wait_recv()
+        ycopy(c, j, 3).start()
 
     r = lax.broadcasted_iota(jnp.int32, (chunk, width), 0) % PACK
 
     def up_part(c):
         for j in range(SIDE):
-            y_arrival(c, j, 2).wait_recv()
-            y_arrival(c, j, 3).wait_recv()
+            for n in (0, 1, 4) if GATHER_DIRECT[c] else (2, 3):
+                y_arrival(c, j, n).wait_recv()
         lhs = jnp.concatenate([ag[c, g] for g in range(SIDE * SIDE)], axis=1)
         u = mm(lhs, wu[...].reshape(SIDE * SIDE * LANES, 3 * width))
         v = u[:, 0:width] + jnp.where(
@@ -252,42 +253,28 @@
         wd[z, 2 * width : 3 * width, pl.ds(to1, LANES)] = jnp.where(left, 0.0, g).astype(BF16)
         return c
 
-    for i in range(1, xs):
-        first_x(i).wait_recv()
-    own_out(0)
-    for i in range(1, xs):
-        other_x(i).wait_recv()
+    pl.semaphore_signal(hint, inc=1, device_id=at_zh(-1))
     across(1).start()
     across(2).start()
-    wu[:, 64:128, width : 2 * width] = jnp.zeros((wu.shape[0], 64, width), BF16)
-    wu[:, 0:64, 2 * width : 3 * width] = jnp.zeros((wu.shape[0], 64, width), BF16)
-    z_out(0)
-    across(1).wait_recv()
-    across(3).start()
-    own_out(1)
-    y_pass(0)
+    to_x(0)
     loads[3].wait()
     lax.fori_loop(0, SIDE, pad_down, 0)
-    z_out(1)
-    across(2).wait_recv()
-    own_out(2)
-    y_pass(1)
-    for c in loads[:3]:
-        c.wait()
-    up_part(0)
-    z_out(2)
-    across(3).wait_recv()
-    own_out(3)
-    y_pass(2)
+    pl.semaphore_wait(hint, 1)
+    across(3).start()
     lax.fori_loop(SIDE, 2 * SIDE, pad_down, 0)
-    up_part(1)
-    z_out(3)
-    y_pass(3)
-    scaled = jnp.concatenate([jnp.where(p, weight, 0.0) for p in puts], axis=0)
-    place[0] = scaled.astype(BF16)
-    place[1] = (scaled - scaled.astype(BF16).astype(F32)).astype(BF16)
-    up_part(2)
-    up_part(3)
+
+    def arrived(c):
+        for i in range(1, xs):
+            over_x(c, i).wait_recv()
+        own_out(c)
+        if c == 0:
+            wu[:, 64:128, width : 2 * width] = jnp.zeros((wu.shape[0], 64, width), BF16)
+            wu[:, 0:64, 2 * width : 3 * width] = jnp.zeros((wu.shape[0], 64, width), BF16)
+            for load in loads[:3]:
+                load.wait()
+            scaled = jnp.concatenate([jnp.where(p, weight, 0.0) for p in puts], axis=0)
+            place[0] = scaled.astype(BF16)
+            place[1] = (scaled - scaled.astype(BF16).astype(F32)).astype(BF16)
 
     def line(c, j, n):
         src, dst, to = (
@@ -295,6 +282,7 @@
             (a_dn, ra_dn, seg_down),
             (b_up, rb_up, seg_up),
             (b_dn, rb_dn, seg_down),
+            (b_far, rb_far, seg_far),
         )[n]
         return pltpu.make_async_remote_copy(
             src_ref=src.at[c, j],
@@ -306,6 +294,15 @@
 
     def down_first(c, j):
         part = mm(hp[c], wd[zpeer[j]])
+        own[c, j] = part[:, 256:384]
+        if SUM_DIRECT[c]:
+            b_far[c, j] = part[:, 0:128].astype(BF16)
+            line(c, j, 4).start()
+            b_up[c, j] = part[:, 384:512].astype(BF16)
+            line(c, j, 2).start()
+            b_dn[c, j] = part[:, 128:256].astype(BF16)
+            line(c, j, 3).start()
+            return
         a_up[c, j] = part[0:half, 0:128].astype(BF16)
         a_dn[c, j] = part[half:chunk, 0:128].astype(BF16)
         line(c, j, 0).start()
@@ -314,7 +311,6 @@
         b_dn[c, j, 0:half] = part[0:half, 128:256].astype(BF16)
         keep_up[c, j] = part[0:half, 384:512]
         keep_dn[c, j] = part[half:chunk, 128:256]
-        own[c, j] = part[:, 256:384]
 
     def down_second(c, j):
         line(c, j, 0).wait_recv()
@@ -337,19 +333,23 @@
         line(c, j, 2).wait_recv()
         line(c, j, 3).wait_recv()
         total = own[c, j] + rb_up[c, j].astype(F32) + rb_dn[c, j].astype(F32)
+        if SUM_DIRECT[c]:
+            line(c, j, 4).wait_recv()
+            total += rb_far[c, j].astype(F32)
         if j:
             zs[c, j] = total.astype(BF16)
             zsum(c, j).start()
         else:
             own[c, j] = total
 
-    def home(c):
-        return pltpu.make_async_remote_copy(
-            src_ref=fb.at[c],
-            dst_ref=rb1.at[c],
-            send_sem=th_s.at[c],
-            recv_sem=th_r.at[c],
-            device_id=at_zh(OFF[c]),
+    def home(c, i):
+        to = (x + i) % xs
+        return pltpu.make_async_remote_copy(
+            src_ref=fb.at[c, pl.ds(to * PACK, PACK)],
+            dst_ref=rb2.at[c, pl.ds(x * PACK, PACK)],
+            send_sem=th_s.at[c, i],
+            recv_sem=th_r.at[c, i],
+            device_id={"expert": (zh + OFF[c]) % SIDE * xs + to},
         )
 
     def finish(c):
@@ -357,66 +357,44 @@
         for j in range(1, SIDE):
             zsum(c, j).wait_recv()
             total += zr[c, j].astype(F32)
-        if c:
-            fb[c] = total.astype(BF16)
-            home(c).start()
-        else:
-            rb1[c] = total.astype(BF16)
-
-    def share(c, i):
-        to = (x + i) % xs
-        return pltpu.make_async_remote_copy(
-            src_ref=rb1.at[c, pl.ds(to * PACK, PACK)],
-            dst_ref=rb2.at[c, pl.ds(x * PACK, PACK)],
-            send_sem=tx_s.at[c, i],
-            recv_sem=tx_r.at[c, i],
-            device_id=at_x(i),
-        )
-
-    def spread(c):
-        if c:
-            home(c).wait_recv()
-        for i in range(1, xs):
-            share(c, i).start()
-        rb2[c, mine, :] = rb1[c, mine, :]
-
-    order = [(c, j) for c in (3, 1, 2, 0) for j in (1, 2, 3, 0)]
-    done = {3: 0, 1: 0, 2: 0, 0: 0}
-    for n in range(len(order) + LAG3 + LAG4):
-        if n < len(order):
-            down_first(*order[n])
-        if 0 <= n - LAG2 < len(order):
-            down_second(*order[n - LAG2])
-        if 0 <= n - LAG3 < len(order):
-            down_third(*order[n - LAG3])
-        m = n - LAG3 - LAG4
-        if 0 <= m < len(order) and m % SIDE == SIDE - 1 and order[m][0]:
-            finish(order[m][0])
-    spread(3)
-    spread(1)
-    finish(0)
-    spread(0)
-    spread(2)
-
-    for i in range(1, xs):
-        first_x(i).wait_send()
-        other_x(i).wait_send()
+        fb[c] = total.astype(BF16)
+        for i in range(c == 0, xs):
+            home(c, i).start()
+        if c == 0:
+            rb2[0, mine, :] = fb[0, mine, :]
+
+    steps = (
+        lambda c, j: arrived(c),
+        z_out,
+        y_pass,
+        lambda c, j: up_part(c),
+        down_first,
+        down_second,
+        down_third,
+        lambda c, j: finish(c),
+        lambda c, j: to_x(c),
+    )
+    for step in ORDER:
+        steps[step // 16](step % 16 // 4, step % 4)
+
     for c in range(SIDE):
         if c:
             across(c).wait_send()
-            home(c).wait_send()
         for i in range(1, xs):
-            share(c, i).wait_send()
+            over_x(c, i).wait_send()
+        for i in range(c == 0, xs):
+            home(c, i).wait_send()
         for j in range(SIDE):
             if j:
                 zcopy(c, j).wait_send()
                 zsum(c, j).wait_send()
-            for n in range(4):
+            for n in (0, 1, 4) if GATHER_DIRECT[c] else range(4):
                 ycopy(c, j, n).wait_send()
+            for n in (2, 3, 4) if SUM_DIRECT[c] else range(4):
                 line(c, j, n).wait_send()
     for c in range(SIDE):
-        for i in range(1, xs):
-            share(c, i).wait_recv()
+        for i in range(c == 0, xs):
+            home(c, i).wait_recv()
     got = rb2[...].reshape(rows, LANES)
     mixed = mm(place[0], got) + mm(place[1], got)
     out_ref[:, 0:128] = mixed[0:tokens].astype(BF16)
@@ -441,7 +419,7 @@
         out_specs=pl.BlockSpec(memory_space=vm),
         scratch_shapes=[
             vm((SIDE, chunk, LANES), BF16),
-            vm((SIDE - 1, chunk, LANES), BF16),
+            vm((SIDE, chunk, LANES), BF16),
             vm((SIDE, segs, chunk, LANES), BF16),
             vm((segs, LANES, 3 * width), BF16),
             vm((width, segs * block), BF16),
@@ -452,8 +430,10 @@
             vm((*each, half, LANES), BF16),
             vm((*each, chunk, LANES), BF16),
             vm((*each, chunk, LANES), BF16),
+            vm((*each, chunk, LANES), BF16),
             vm((*each, half, LANES), BF16),
             vm((*each, half, LANES), BF16),
+            vm((*each, chunk, LANES), BF16),
             vm((*each, chunk, LANES), BF16),
             vm((*each, chunk, LANES), BF16),
             vm((*each, half, LANES), F32),
@@ -463,22 +443,20 @@
             vm((*each, chunk, LANES), BF16),
             vm((SIDE, chunk, LANES), BF16),
             vm((SIDE, chunk, LANES), BF16),
-            vm((SIDE, chunk, LANES), BF16),
             dma((4,)),
-            dma((2, xs)),
-            dma((2, xs)),
+            pltpu.SemaphoreType.REGULAR,
+            dma((SIDE, xs)),
+            dma((SIDE, xs)),
             dma((SIDE,)),
             dma((SIDE,)),
             dma(each),
             dma(each),
-            dma((*each, 4)),
-            dma((*each, 4)),
-            dma((*each, 4)),
-            dma((*each, 4)),
+            dma((*each, 5)),
+            dma((*each, 5)),
+            dma((*each, 5)),
+            dma((*each, 5)),
             dma(each),
             dma(each),
-            dma((SIDE,)),
-            dma((SIDE,)),
             dma((SIDE, xs)),
             dma((SIDE, xs)),
         ],

time: 88.2 us -> 78.7 us (0.89)
  the two profiles are of different devices: /device:TPU:2 before, /device:TPU:32 now
where the time goes in v3:
time: 78.7 us; the launch traced here: 78.4 us
  Pallas kernels  77 us (98%)
  local copies, waits for them, and re-layouts  1.38 us (2%)
    pallas_call x1, Pallas kernels, shards(): pl.pallas_call(functools.partial(layer, experts), out_shape=jax.ShapeDtyp...  77 us

profile of v3, /device:TPU:32, one launch (start us, length us, event | category | flops | bytes accessed | tf_op | source)
XLA Modules:
  0.0 78.4 jit_solution(13532032441200629915)
XLA Ops:
  0.0 77.0 %shard_map.55 = bf16[64,192]{1,0:T(8,128)(2,1)} custom-call(bf16[64,192]{1,0:T(8,128)(2,1)} %tok_ref.1, s32[4,64]{1,0:T(4,128)} %bitcast.6, f32[4,64]{1,0:T(4,128)} %bitcast.7, bf16[16,192,384]{2,1,0:T(8,128)(2,1)} %bitcast.4, bf16[384,3072]{1,0:T(8,128)(2,1)} %bitcast.5), custom_call_target="tpu_custom_call" | custom-call | tf_op jit(solution)/shard_map/pallas_call | solution.py:415
  77.0 1.4 %copy.7 = bf16[64,192]{1,0:T(8,128)(2,1)} copy(bf16[64,192]{1,0:T(8,128)(2,1)} %shard_map.55) | data formatting | bytes 49152

commit v4 on v3

--- a/solution.py
+++ b/solution.py
@@ -12,15 +12,15 @@
 LANES = 128
 SIDE = 4
 OFF = (0, 1, 3, 2)
-GATHER_DIRECT = (0, 0, 0, 0)
-SUM_DIRECT = (0, 0, 0, 0)
+GATHER_DIRECT = (1, 0, 0, 0)
+SUM_DIRECT = (0, 0, 0, 1)
 ORDER = (
-    0, 132, 136, 32, 17, 4, 8, 18, 140, 19, 33, 36, 21, 40, 34, 12,
-    35, 22, 23, 25, 37, 26, 44, 27, 48, 29, 38, 39, 30, 41, 31, 42,
-    43, 45, 52, 46, 69, 70, 47, 71, 56, 68, 85, 86, 60, 87, 77, 78,
-    84, 79, 76, 101, 73, 74, 102, 75, 72, 65, 103, 93, 66, 94, 67, 100,
-    64, 95, 92, 89, 90, 91, 88, 81, 109, 82, 116, 110, 83, 80, 111, 108,
-    105, 106, 107, 104, 97, 124, 98, 99, 96, 120, 112,
+    0, 132, 136, 17, 48, 4, 8, 18, 19, 140, 49, 36, 21, 40, 22, 50,
+    23, 12, 25, 52, 51, 37, 26, 56, 38, 27, 39, 44, 29, 41, 53, 30,
+    42, 54, 31, 43, 55, 69, 70, 45, 71, 68, 46, 60, 57, 58, 47, 59,
+    85, 73, 86, 74, 87, 75, 84, 72, 61, 62, 63, 77, 101, 89, 78, 79,
+    102, 90, 76, 65, 103, 91, 66, 67, 100, 88, 64, 109, 105, 110, 116, 111,
+    106, 108, 81, 107, 82, 83, 104, 124, 80, 97, 98, 99, 120, 96,
 )
 F32 = jnp.float32
 BF16 = jnp.bfloat16
@@ -35,10 +35,10 @@
 
 
 def layer(
-    experts, tok_ref, ids_ref, rw_ref, wup_ref, wdn_ref, out_ref,
-    sbuf, mid, ag, wu, wraw, wd, hp, place, a_up, a_dn, b_up, b_dn, b_far, ra_up, ra_dn, rb_up, rb_dn, rb_far,
-    keep_up, keep_dn, own, zs, zr, fb, rb2,
-    wsem, hint, dx_s, dx_r, dz_s, dz_r, z_s, z_r, y_s, y_r, r_s, r_r, zz_s, zz_r, th_s, th_r,
+    experts, tok_hbm, ids_hbm, rw_hbm, wup_ref, wdn_ref, out_ref,
+    tok_ref, ids_ref, rw_ref, sbuf, mid, ag, wu, wraw, wd, acc, hp, place, a_up, a_dn, b_up, b_dn, b_far, ra_up, ra_dn, rb_up, rb_dn, rb_far,
+    keep_up, keep_dn, own, zs, zr, fb, rb0, rb2,
+    isem, wsem, hint, dx_s, dx_r, dz_s, dz_r, z_s, z_r, y_s, y_r, r_s, r_r, zz_s, zz_r, th_s, th_r, t0_s, t0_r,
 ):
     topk = ids_ref.shape[0]
     tokens = tok_ref.shape[0]
@@ -63,6 +63,13 @@
     def at_x(i):
         return {"expert": zh * xs + (x + i) % xs}
 
+    small = [
+        pltpu.make_async_copy(tok_hbm, tok_ref, isem.at[0]),
+        pltpu.make_async_copy(ids_hbm, ids_ref, isem.at[1]),
+        pltpu.make_async_copy(rw_hbm, rw_ref, isem.at[2]),
+    ]
+    for c in small:
+        c.start()
     barrier = pltpu.get_barrier_semaphore()
     near = [at_x(i) for i in range(1, xs)] + [at_zh(1), at_zh(-1)]
     near += [{"seg": seg_up}, {"seg": seg_down}, {"seg": seg_far}]
@@ -79,6 +86,8 @@
     for c in loads:
         c.start()
 
+    for c in small:
+        c.wait()
     table = jnp.concatenate([ids_ref[...].astype(F32), rw_ref[...]], axis=0).T
     ids, rw = table[:, 0:topk], table[:, topk : 2 * topk]
     norm = rw / jnp.sum(rw, axis=1, keepdims=True)
@@ -218,12 +227,20 @@
 
     r = lax.broadcasted_iota(jnp.int32, (chunk, width), 0) % PACK
 
-    def up_part(c):
-        for j in range(SIDE):
-            for n in (0, 1, 4) if GATHER_DIRECT[c] else (2, 3):
-                y_arrival(c, j, n).wait_recv()
-        lhs = jnp.concatenate([ag[c, g] for g in range(SIDE * SIDE)], axis=1)
-        u = mm(lhs, wu[...].reshape(SIDE * SIDE * LANES, 3 * width))
+    summed = [0] * SIDE
+
+    def up_part(c, j):
+        for n in (0, 1, 4) if GATHER_DIRECT[c] else (2, 3):
+            y_arrival(c, j, n).wait_recv()
+        g = zpeer[j] * SIDE
+        lhs = jnp.concatenate([ag[c, g + i] for i in range(SIDE)], axis=1)
+        u = mm(lhs, wu[pl.ds(g, SIDE)].reshape(SIDE * LANES, 3 * width))
+        if summed[c]:
+            u += acc[c]
+        summed[c] += 1
+        if summed[c] < SIDE:
+            acc[c] = u
+            return
         v = u[:, 0:width] + jnp.where(
             r < 11,
             pltpu.roll(u[:, width : 2 * width], chunk - 21, 0),
@@ -320,6 +337,12 @@
         b_dn[c, j, half:chunk] = (keep_dn[c, j] + ra_dn[c, j].astype(F32)).astype(BF16)
         line(c, j, 3).start()
 
+    def gather_left(c, j):
+        if j:
+            zcopy(c, j).wait_send()
+        for n in (0, 1, 4) if GATHER_DIRECT[c] else range(4):
+            ycopy(c, j, n).wait_send()
+
     def zsum(c, j):
         return pltpu.make_async_remote_copy(
             src_ref=zs.at[c, j],
@@ -329,14 +352,31 @@
             device_id={"seg": zpeer[j] * SIDE + y},
         )
 
+    def straight(j, i):
+        to = (x + i) % xs
+        return pltpu.make_async_remote_copy(
+            src_ref=zs.at[0, j, pl.ds(to * PACK, PACK)],
+            dst_ref=rb0.at[j, pl.ds(x * PACK, PACK)],
+            send_sem=t0_s.at[j, i],
+            recv_sem=t0_r.at[j, i],
+            device_id={"expert": zh * xs + to, "seg": zpeer[j] * SIDE + y},
+        )
+
     def down_third(c, j):
         line(c, j, 2).wait_recv()
         line(c, j, 3).wait_recv()
+        gather_left(c, j)
         total = own[c, j] + rb_up[c, j].astype(F32) + rb_dn[c, j].astype(F32)
         if SUM_DIRECT[c]:
             line(c, j, 4).wait_recv()
             total += rb_far[c, j].astype(F32)
-        if j:
+        if c == 0:
+            zs[0, j] = total.astype(BF16)
+            for i in range(j == 0, xs):
+                straight(j, i).start()
+            if j == 0:
+                rb0[0, mine, :] = zs[0, 0, mine, :]
+        elif j:
             zs[c, j] = total.astype(BF16)
             zsum(c, j).start()
         else:
@@ -358,16 +398,14 @@
             zsum(c, j).wait_recv()
             total += zr[c, j].astype(F32)
         fb[c] = total.astype(BF16)
-        for i in range(c == 0, xs):
+        for i in range(xs):
             home(c, i).start()
-        if c == 0:
-            rb2[0, mine, :] = fb[0, mine, :]
 
     steps = (
         lambda c, j: arrived(c),
         z_out,
         y_pass,
-        lambda c, j: up_part(c),
+        up_part,
         down_first,
         down_second,
         down_third,
@@ -382,19 +420,25 @@
             across(c).wait_send()
         for i in range(1, xs):
             over_x(c, i).wait_send()
-        for i in range(c == 0, xs):
+        for i in range(xs if c else 0):
             home(c, i).wait_send()
         for j in range(SIDE):
-            if j:
-                zcopy(c, j).wait_send()
+            if c == 0:
+                for i in range(j == 0, xs):
+                    straight(j, i).wait_send()
+            elif j:
                 zsum(c, j).wait_send()
-            for n in (0, 1, 4) if GATHER_DIRECT[c] else range(4):
-                ycopy(c, j, n).wait_send()
             for n in (2, 3, 4) if SUM_DIRECT[c] else range(4):
                 line(c, j, n).wait_send()
-    for c in range(SIDE):
-        for i in range(c == 0, xs):
+    for c in range(1, SIDE):
+        for i in range(xs):
             home(c, i).wait_recv()
+    total = jnp.zeros((chunk, LANES), F32)
+    for j in range(SIDE):
+        for i in range(j == 0, xs):
+            straight(j, i).wait_recv()
+        total += rb0[j].astype(F32)
+    rb2[0] = total.astype(BF16)
     got = rb2[...].reshape(rows, LANES)
     mixed = mm(place[0], got) + mm(place[1], got)
     out_ref[:, 0:128] = mixed[0:tokens].astype(BF16)
@@ -415,15 +459,19 @@
     return pl.pallas_call(
         functools.partial(layer, experts),
         out_shape=jax.ShapeDtypeStruct(tokens.shape, BF16),
-        in_specs=[pl.BlockSpec(memory_space=vm)] * 3 + [pl.BlockSpec(memory_space=pl.ANY)] * 2,
+        in_specs=[pl.BlockSpec(memory_space=pl.ANY)] * 5,
         out_specs=pl.BlockSpec(memory_space=vm),
         scratch_shapes=[
+            vm(tokens.shape, BF16),
+            vm(expert_ids.shape[::-1], jnp.int32),
+            vm(route_weight.shape[::-1], F32),
             vm((SIDE, chunk, LANES), BF16),
             vm((SIDE, chunk, LANES), BF16),
             vm((SIDE, segs, chunk, LANES), BF16),
             vm((segs, LANES, 3 * width), BF16),
             vm((width, segs * block), BF16),
             vm((SIDE, 3 * width, SIDE * LANES), BF16),
+            vm((SIDE, chunk, 3 * width), F32),
             vm((SIDE, chunk, 3 * width), BF16),
             vm((2, 3 * count, SIDE * chunk), BF16),
             vm((*each, half, LANES), BF16),
@@ -443,6 +491,8 @@
             vm((*each, chunk, LANES), BF16),
             vm((SIDE, chunk, LANES), BF16),
             vm((SIDE, chunk, LANES), BF16),
+            vm((SIDE, chunk, LANES), BF16),
+            dma((3,)),
             dma((4,)),
             pltpu.SemaphoreType.REGULAR,
             dma((SIDE, xs)),
@@ -459,6 +509,8 @@
             dma(each),
             dma((SIDE, xs)),
             dma((SIDE, xs)),
+            dma((SIDE, xs)),
+            dma((SIDE, xs)),
         ],
         compiler_params=pltpu.CompilerParams(
             collective_id=0, has_side_effects=True, vmem_limit_bytes=56 * 2**20

time: 78.7 us -> 76.8 us (0.976)
  the two profiles are of different devices: /device:TPU:32 before, /device:TPU:64 now
where the time goes in v4:
time: 76.8 us; the launch traced here: 76.6 us
  Pallas kernels  75.2 us (98%)
  local copies, waits for them, and re-layouts  1.38 us (2%)
    pallas_call x1, Pallas kernels, shards(): pl.pallas_call(functools.partial(layer, experts), out_shape=jax.ShapeDtyp...  75.2 us

profile of v4, /device:TPU:64, one launch (start us, length us, event | category | flops | bytes accessed | tf_op | source)
XLA Modules:
  0.0 76.6 jit_solution(8348215947398505009)
XLA Ops:
  0.0 75.2 %shard_map.55 = bf16[64,192]{1,0:T(8,128)(2,1)} custom-call(bf16[64,192]{1,0:T(8,128)(2,1)} %tok_hbm.1, s32[4,64]{1,0:T(4,128)} %bitcast.6, f32[4,64]{1,0:T(4,128)} %bitcast.7, bf16[16,192,384]{2,1,0:T(8,128)(2,1)} %bitcast.4, bf16[384,3072]{1,0:T(8,128)(2,1)} %bitcast.5), custom_call_target="tpu_custom_call" | custom-call | tf_op jit(solution)/shard_map/pallas_call | solution.py:459
  75.2 1.4 %copy.7 = bf16[64,192]{1,0:T(8,128)(2,1)} copy(bf16[64,192]{1,0:T(8,128)(2,1)} %shard_map.55) | data formatting | bytes 49152

commit v5 on v4

--- a/solution.py
+++ b/solution.py
@@ -71,7 +71,7 @@
     for c in small:
         c.start()
     barrier = pltpu.get_barrier_semaphore()
-    near = [at_x(i) for i in range(1, xs)] + [at_zh(1), at_zh(-1)]
+    near = [at_zh(1), at_zh(-1)] + [at_x(i) for i in range(1, xs)]
     near += [{"seg": seg_up}, {"seg": seg_down}, {"seg": seg_far}]
     near += [{"seg": zpeer[j] * SIDE + y} for j in range(1, SIDE)]
     for to in near:
@@ -392,6 +392,20 @@
             device_id={"expert": (zh + OFF[c]) % SIDE * xs + to},
         )
 
+    def sums_left(c):
+        if c:
+            across(c).wait_send()
+        for i in range(1, xs):
+            over_x(c, i).wait_send()
+        for j in range(SIDE):
+            if c == 0:
+                for i in range(j == 0, xs):
+                    straight(j, i).wait_send()
+            elif j:
+                zsum(c, j).wait_send()
+            for n in (2, 3, 4) if SUM_DIRECT[c] else range(4):
+                line(c, j, n).wait_send()
+
     def finish(c):
         total = own[c, 0]
         for j in range(1, SIDE):
@@ -400,6 +414,7 @@
         fb[c] = total.astype(BF16)
         for i in range(xs):
             home(c, i).start()
+        sums_left(c)
 
     steps = (
         lambda c, j: arrived(c),
@@ -415,21 +430,10 @@
     for step in ORDER:
         steps[step // 16](step % 16 // 4, step % 4)
 
-    for c in range(SIDE):
-        if c:
-            across(c).wait_send()
-        for i in range(1, xs):
-            over_x(c, i).wait_send()
-        for i in range(xs if c else 0):
+    sums_left(0)
+    for c in range(1, SIDE):
+        for i in range(xs):
             home(c, i).wait_send()
-        for j in range(SIDE):
-            if c == 0:
-                for i in range(j == 0, xs):
-                    straight(j, i).wait_send()
-            elif j:
-                zsum(c, j).wait_send()
-            for n in (2, 3, 4) if SUM_DIRECT[c] else range(4):
-                line(c, j, n).wait_send()
     for c in range(1, SIDE):
         for i in range(xs):
             home(c, i).wait_recv()

time: 76.8 us -> 76.4 us (level)
  no operation moved by 1% of the time
where the time goes in v5:
time: 76.4 us; the launch traced here: 76.2 us
  Pallas kernels  74.8 us (98%)
  local copies, waits for them, and re-layouts  1.38 us (2%)
    pallas_call x1, Pallas kernels, shards(): pl.pallas_call(functools.partial(layer, experts), out_shape=jax.ShapeDtyp...  74.8 us

profile of v5, /device:TPU:64, one launch (start us, length us, event | category | flops | bytes accessed | tf_op | source)
XLA Modules:
  0.0 76.2 jit_solution(14107664404636559367)
XLA Ops:
  0.0 74.8 %shard_map.55 = bf16[64,192]{1,0:T(8,128)(2,1)} custom-call(bf16[64,192]{1,0:T(8,128)(2,1)} %tok_hbm.1, s32[4,64]{1,0:T(4,128)} %bitcast.6, f32[4,64]{1,0:T(4,128)} %bitcast.7, bf16[16,192,384]{2,1,0:T(8,128)(2,1)} %bitcast.4, bf16[384,3072]{1,0:T(8,128)(2,1)} %bitcast.5), custom_call_target="tpu_custom_call" | custom-call | tf_op jit(solution)/shard_map/pallas_call | solution.py:463
  74.8 1.4 %copy.7 = bf16[64,192]{1,0:T(8,128)(2,1)} copy(bf16[64,192]{1,0:T(8,128)(2,1)} %shard_map.55) | data formatting | bytes 49152
